TPU v7x, 1024 devices: a whole 4x4x32 slice. The times are simulated.
1024 devices in a mesh: blk: 256 (over z_lo, x, y), grp: 4 (over z_hi, core).
Axes of the slice: x: 4, y: 4, z: 32 (z_hi: 2, z_lo: 16; z = z_hi * 16 + z_lo), core: 2. Of those that a mesh axis runs over, the one named last changes fastest.
Arguments:
- image_emb: float32 [131072, 1152], P(('blk', 'grp')), may hold values from -0.1875 to 0.1875
- text_emb: float32 [131072, 1152], P(('blk', 'grp')), may hold values from -0.1875 to 0.1875
- log_scale: float32 [1], replicated, may hold values from 1.5 to 2.5
- bias: float32 [1], replicated, may hold values from -3 to 0
Outputs:
- row_loss: float32 [131072], P(('blk', 'grp'))
- image_grad: float32 [131072, 1152], P(('blk', 'grp'))
- text_grad: float32 [131072, 1152], P(('blk', 'grp'))
All inputs are finite; a program needn't handle non-finite values.
Results may differ from a plain program's by a relative error of at most 0.012.
Values may be sent and summed in bfloat16 or wider, within the bound.
A program may use at most 32 MiB of HBM per device.

v0:
```python
import jax
import jax.numpy as jnp
from jax import lax
from jax.sharding import PartitionSpec as P

SPAN = 4


def passed_along(x, axis, by):
    devices = lax.axis_size(axis)
    return lax.ppermute(x, axis, [(i, (i + by) % devices) for i in range(devices)])


def unit_rows(emb):
    norms = jnp.sqrt(jnp.sum(emb * emb, axis=1, keepdims=True) + 1e-06)
    return (emb / norms, norms)


def unit_backward(unit, norms, grad):
    return (grad - unit * jnp.sum(unit * grad, axis=1, keepdims=True)) / norms


def on_device(image_emb, text_emb, log_scale, bias):
    rows = image_emb.shape[0]
    scale = jnp.exp(log_scale[0])
    offset = bias[0]
    image_unit, image_norm = unit_rows(image_emb)
    text_unit, text_norm = unit_rows(text_emb)
    image_half = image_unit.astype(jnp.bfloat16)
    text_half = text_unit.astype(jnp.bfloat16)
    diagonal = 2.0 * jnp.eye(rows, dtype=jnp.float32) - 1.0
    negative = jnp.float32(-1.0)
    held = passed_along(text_half, ("blk", "grp"), -SPAN)
    carried = jnp.zeros((rows, text_half.shape[1]), jnp.float32)
    loss_total = jnp.zeros((rows,), jnp.float32)
    image_acc = jnp.zeros((rows, image_half.shape[1]), jnp.float32)
    for step in range(2 * SPAN + 1):
        signs = diagonal if step == SPAN else negative
        logits = (
            scale
            * lax.dot_general(
                image_half, held, (((1,), (1,)), ((), ())), preferred_element_type=jnp.float32
            )
            + offset
        )
        coeff = (-scale * signs * jax.nn.sigmoid(-signs * logits)).astype(jnp.bfloat16)
        loss_part = jnp.sum(jax.nn.softplus(-signs * logits), axis=1)
        image_part = jnp.dot(coeff, held, preferred_element_type=jnp.float32)
        text_part = lax.dot_general(
            coeff, image_half, (((0,), (0,)), ((), ())), preferred_element_type=jnp.float32
        )
        loss_part, image_part, text_part = (loss_part, image_part, text_part)
        loss_total = loss_total + loss_part
        image_acc = image_acc + image_part
        carried = carried + text_part
        if step < 2 * SPAN:
            held, carried = (
                passed_along(held.astype(jnp.float32), ("blk", "grp"), 1).astype(held.dtype),
                passed_along(carried, ("blk", "grp"), 1),
            )
    text_acc = passed_along(carried.astype(jnp.bfloat16), ("blk", "grp"), -SPAN).astype(
        carried.dtype
    )
    row_loss = loss_total / ((2 * SPAN + 1) * rows)
    image_grad = unit_backward(image_unit, image_norm, image_acc)
    text_grad = unit_backward(text_unit, text_norm, text_acc)
    return (row_loss, image_grad, text_grad)


def solution(mesh):
    in_specs = (P(("blk", "grp"), None), P(("blk", "grp"), None), P(), P())
    out_specs = (P(("blk", "grp")), P(("blk", "grp"), None), P(("blk", "grp"), None))
    return jax.shard_map(
        on_device, mesh=mesh, in_specs=in_specs, out_specs=out_specs, check_vma=False
    )
```

profile of v0, /device:TPU:32, one launch (start us, length us, event | category | flops | bytes accessed | tf_op | source)
XLA Modules:
  0.0 1262.3 jit_solution(13555202396300183896)
XLA Ops:
  2.0 6.8 collective-permute-start
  10.4 4.6 collective-permute-done
  17.5 29.1 %collective-permute-start.9 = (f32[128,1152]{1,0:T(8,128)S(1)}, f32[128,1152]{1,0:T(8,128)S(1)}, u32[]{:S(2)}, u32[]{:S(2)}) collective-permute-start(f32[128,1152]{1,0:T(8,128)S(1)} %fusion.52), channel_id=1, source_target_pairs={{0,1},{1,2},{2,3},{3,4},{4,5},{5,6},{6,7},{7,8},{8,9},{9,10},{10,1... | collective-permute-start | bytes 1769480 | tf_op jit(solution)/shard_map/ppermute | solution.py:11
  46.6 140.1 %collective-permute-done.1 = bf16[128,1152]{1,0:T(8,128)(2,1)S(1)} collective-permute-done((bf16[128,1152]{1,0:T(8,128)(2,1)S(1)}, bf16[128,1152]{1,0:T(8,128)(2,1)S(1)}, u32[]{:S(2)}, u32[]{:S(2)}) %collective-permute-start.1) | collective-permute-done | bytes 294944 | tf_op jit(solution)/shard_map/ppermute | solution.py:11
  189.2 250.4 %collective-permute-done.9 = f32[128,1152]{1,0:T(8,128)S(1)} collective-permute-done((f32[128,1152]{1,0:T(8,128)S(1)}, f32[128,1152]{1,0:T(8,128)S(1)}, u32[]{:S(2)}, u32[]{:S(2)}) %collective-permute-start.9) | collective-permute-done | bytes 589856 | tf_op jit(solution)/shard_map/ppermute | solution.py:11
  439.9 1.9 collective-permute-start.10
  441.8 56.2 %collective-permute-done.2 = bf16[128,1152]{1,0:T(8,128)(2,1)S(1)} collective-permute-done((bf16[128,1152]{1,0:T(8,128)(2,1)S(1)}, bf16[128,1152]{1,0:T(8,128)(2,1)S(1)}, u32[]{:S(2)}, u32[]{:S(2)}) %collective-permute-start.2) | collective-permute-done | bytes 294944 | tf_op jit(solution)/shard_map/ppermute | solution.py:11
  500.8 496.4 %collective-permute-done.3 = bf16[128,1152]{1,0:T(8,128)(2,1)S(1)} collective-permute-done((bf16[128,1152]{1,0:T(8,128)(2,1)S(1)}, bf16[128,1152]{1,0:T(8,128)(2,1)S(1)}, u32[]{:S(2)}, u32[]{:S(2)}) %collective-permute-start.3) | collective-permute-done | bytes 294944 | tf_op jit(solution)/shard_map/ppermute | solution.py:11
  999.7 1.9 collective-permute-start.11
  1001.9 43.5 %collective-permute-done.4 = bf16[128,1152]{1,0:T(8,128)(2,1)S(1)} collective-permute-done((bf16[128,1152]{1,0:T(8,128)(2,1)S(1)}, bf16[128,1152]{1,0:T(8,128)(2,1)S(1)}, u32[]{:S(2)}, u32[]{:S(2)}) %collective-permute-start.4) | collective-permute-done | bytes 294944 | tf_op jit(solution)/shard_map/ppermute | solution.py:11
  1047.9 32.6 %collective-permute-done.11 = f32[128,1152]{1,0:T(8,128)S(1)} collective-permute-done((f32[128,1152]{1,0:T(8,128)S(1)}, f32[128,1152]{1,0:T(8,128)S(1)}, u32[]{:S(2)}, u32[]{:S(2)}) %collective-permute-start.11) | collective-permute-done | bytes 589856 | tf_op jit(solution)/shard_map/ppermute | solution.py:11
  1080.6 1.9 collective-permute-start.12
  1086.2 34.3 %collective-permute-done.12 = f32[128,1152]{1,0:T(8,128)S(1)} collective-permute-done((f32[128,1152]{1,0:T(8,128)S(1)}, f32[128,1152]{1,0:T(8,128)S(1)}, u32[]{:S(2)}, u32[]{:S(2)}) %collective-permute-start.12) | collective-permute-done | bytes 589856 | tf_op jit(solution)/shard_map/ppermute | solution.py:11
  1120.5 1.9 collective-permute-start.13
  1122.8 23.0 %collective-permute-done.6 = bf16[128,1152]{1,0:T(8,128)(2,1)S(1)} collective-permute-done((bf16[128,1152]{1,0:T(8,128)(2,1)S(1)}, bf16[128,1152]{1,0:T(8,128)(2,1)S(1)}, u32[]{:S(2)}, u32[]{:S(2)}) %collective-permute-start.6) | collective-permute-done | bytes 294944 | tf_op jit(solution)/shard_map/ppermute | solution.py:11
  1148.2 5.3 collective-permute-done.13
  1153.6 1.9 collective-permute-start.14
  1155.8 24.4 %collective-permute-done.7 = bf16[128,1152]{1,0:T(8,128)(2,1)S(1)} collective-permute-done((bf16[128,1152]{1,0:T(8,128)(2,1)S(1)}, bf16[128,1152]{1,0:T(8,128)(2,1)S(1)}, u32[]{:S(2)}, u32[]{:S(2)}) %collective-permute-start.7) | collective-permute-done | bytes 294944 | tf_op jit(solution)/shard_map/ppermute | solution.py:11
  1182.6 3.9 collective-permute-done.14
  1186.5 1.9 collective-permute-start.15
  1188.7 24.4 %collective-permute-done.8 = bf16[128,1152]{1,0:T(8,128)(2,1)S(1)} collective-permute-done((bf16[128,1152]{1,0:T(8,128)(2,1)S(1)}, bf16[128,1152]{1,0:T(8,128)(2,1)S(1)}, u32[]{:S(2)}, u32[]{:S(2)}) %collective-permute-start.8) | collective-permute-done | bytes 294944 | tf_op jit(solution)/shard_map/ppermute | solution.py:11
  1213.7 5.8 collective-permute-done.15
  1222.4 30.0 %collective-permute-done.16 = f32[128,1152]{1,0:T(8,128)S(1)} collective-permute-done((f32[128,1152]{1,0:T(8,128)S(1)}, f32[128,1152]{1,0:T(8,128)S(1)}, u32[]{:S(2)}, u32[]{:S(2)}) %collective-permute-start.16) | collective-permute-done | bytes 589856 | tf_op jit(solution)/shard_map/ppermute | solution.py:11
  1255.9 5.2 collective-permute-done.17
  (60 shorter events, 32.4 us)
Async XLA Ops:
  0.6 1.3 copy-start.1
  1.9 6.9 copy-start
  2.0 13.0 %collective-permute-start = (bf16[128,1152]{1,0:T(8,128)(2,1)S(1)}, bf16[128,1152]{1,0:T(8,128)(2,1)S(1)}, u32[]{:S(2)}, u32[]{:S(2)}) collective-permute-start(bf16[128,1152]{1,0:T(8,128)(2,1)S(1)} %fusion.61), channel_id=1, source_target_pairs={{0,1020},{1,1021},{2,1022},{3,1023},{4,0},{5,1},{6,2},{7,3},{8,4},... | collective-permute-start | bytes 884744 | tf_op jit(solution)/shard_map/ppermute | solution.py:11
  15.1 171.6 %collective-permute-start.1 = (bf16[128,1152]{1,0:T(8,128)(2,1)S(1)}, bf16[128,1152]{1,0:T(8,128)(2,1)S(1)}, u32[]{:S(2)}, u32[]{:S(2)}) collective-permute-start(bf16[128,1152]{1,0:T(8,128)(2,1)S(1)} %collective-permute-done), channel_id=1, source_target_pairs={{0,1},{1,2},{2,3},{3,4},{4,5},{5,6},{6,7},{7,8},{8,9},{9,10},{10,1... | collective-permute-start | bytes 884744 | tf_op jit(solution)/shard_map/ppermute | solution.py:11
  17.5 422.1 %collective-permute-start.9 = (f32[128,1152]{1,0:T(8,128)S(1)}, f32[128,1152]{1,0:T(8,128)S(1)}, u32[]{:S(2)}, u32[]{:S(2)}) collective-permute-start(f32[128,1152]{1,0:T(8,128)S(1)} %fusion.52), channel_id=1, source_target_pairs={{0,1},{1,2},{2,3},{3,4},{4,5},{5,6},{6,7},{7,8},{8,9},{9,10},{10,1... | collective-permute-start | bytes 1769480 | tf_op jit(solution)/shard_map/ppermute | solution.py:11
  186.7 311.3 %collective-permute-start.2 = (bf16[128,1152]{1,0:T(8,128)(2,1)S(1)}, bf16[128,1152]{1,0:T(8,128)(2,1)S(1)}, u32[]{:S(2)}, u32[]{:S(2)}) collective-permute-start(bf16[128,1152]{1,0:T(8,128)(2,1)S(1)} %collective-permute-done.1), channel_id=1, source_target_pairs={{0,1},{1,2},{2,3},{3,4},{4,5},{5,6},{6,7},{7,8},{8,9},{9,10},{10,1... | collective-permute-start | bytes 884744 | tf_op jit(solution)/shard_map/ppermute | solution.py:11
  439.9 559.7 %collective-permute-start.10 = (f32[128,1152]{1,0:T(8,128)S(1)}, f32[128,1152]{1,0:T(8,128)S(1)}, u32[]{:S(2)}, u32[]{:S(2)}) collective-permute-start(f32[128,1152]{1,0:T(8,128)S(1)} %convolution_add_fusion), channel_id=1, source_target_pairs={{0,1},{1,2},{2,3},{3,4},{4,5},{5,6},{6,7},{7,8},{8,9},{9,10},{10,1... | collective-permute-start | bytes 1769480 | tf_op jit(solution)/shard_map/ppermute | solution.py:11
  498.0 499.1 %collective-permute-start.3 = (bf16[128,1152]{1,0:T(8,128)(2,1)S(1)}, bf16[128,1152]{1,0:T(8,128)(2,1)S(1)}, u32[]{:S(2)}, u32[]{:S(2)}) collective-permute-start(bf16[128,1152]{1,0:T(8,128)(2,1)S(1)} %collective-permute-done.2), channel_id=1, source_target_pairs={{0,1},{1,2},{2,3},{3,4},{4,5},{5,6},{6,7},{7,8},{8,9},{9,10},{10,1... | collective-permute-start | bytes 884744 | tf_op jit(solution)/shard_map/ppermute | solution.py:11
  997.2 48.3 %collective-permute-start.4 = (bf16[128,1152]{1,0:T(8,128)(2,1)S(1)}, bf16[128,1152]{1,0:T(8,128)(2,1)S(1)}, u32[]{:S(2)}, u32[]{:S(2)}) collective-permute-start(bf16[128,1152]{1,0:T(8,128)(2,1)S(1)} %collective-permute-done.3), channel_id=1, source_target_pairs={{0,1},{1,2},{2,3},{3,4},{4,5},{5,6},{6,7},{7,8},{8,9},{9,10},{10,1... | collective-permute-start | bytes 884744 | tf_op jit(solution)/shard_map/ppermute | solution.py:11
  999.7 80.8 %collective-permute-start.11 = (f32[128,1152]{1,0:T(8,128)S(1)}, f32[128,1152]{1,0:T(8,128)S(1)}, u32[]{:S(2)}, u32[]{:S(2)}) collective-permute-start(f32[128,1152]{1,0:T(8,128)S(1)} %add.229), channel_id=1, source_target_pairs={{0,1},{1,2},{2,3},{3,4},{4,5},{5,6},{6,7},{7,8},{8,9},{9,10},{10,1... | collective-permute-start | bytes 1769480 | tf_op jit(solution)/shard_map/ppermute | solution.py:11
  1045.5 38.2 %collective-permute-start.5 = (bf16[128,1152]{1,0:T(8,128)(2,1)S(1)}, bf16[128,1152]{1,0:T(8,128)(2,1)S(1)}, u32[]{:S(2)}, u32[]{:S(2)}) collective-permute-start(bf16[128,1152]{1,0:T(8,128)(2,1)S(1)} %collective-permute-done.4), channel_id=1, source_target_pairs={{0,1},{1,2},{2,3},{3,4},{4,5},{5,6},{6,7},{7,8},{8,9},{9,10},{10,1... | collective-permute-start | bytes 884744 | tf_op jit(solution)/shard_map/ppermute | solution.py:11
  1080.6 39.9 %collective-permute-start.12 = (f32[128,1152]{1,0:T(8,128)S(1)}, f32[128,1152]{1,0:T(8,128)S(1)}, u32[]{:S(2)}, u32[]{:S(2)}) collective-permute-start(f32[128,1152]{1,0:T(8,128)S(1)} %add.230), channel_id=1, source_target_pairs={{0,1},{1,2},{2,3},{3,4},{4,5},{5,6},{6,7},{7,8},{8,9},{9,10},{10,1... | collective-permute-start | bytes 1769480 | tf_op jit(solution)/shard_map/ppermute | solution.py:11
  1083.7 62.1 %collective-permute-start.6 = (bf16[128,1152]{1,0:T(8,128)(2,1)S(1)}, bf16[128,1152]{1,0:T(8,128)(2,1)S(1)}, u32[]{:S(2)}, u32[]{:S(2)}) collective-permute-start(bf16[128,1152]{1,0:T(8,128)(2,1)S(1)} %collective-permute-done.5), channel_id=1, source_target_pairs={{0,1},{1,2},{2,3},{3,4},{4,5},{5,6},{6,7},{7,8},{8,9},{9,10},{10,1... | collective-permute-start | bytes 884744 | tf_op jit(solution)/shard_map/ppermute | solution.py:11
  1120.5 32.9 %collective-permute-start.13 = (f32[128,1152]{1,0:T(8,128)S(1)}, f32[128,1152]{1,0:T(8,128)S(1)}, u32[]{:S(2)}, u32[]{:S(2)}) collective-permute-start(f32[128,1152]{1,0:T(8,128)S(1)} %add.231), channel_id=1, source_target_pairs={{0,1},{1,2},{2,3},{3,4},{4,5},{5,6},{6,7},{7,8},{8,9},{9,10},{10,1... | collective-permute-start | bytes 1769480 | tf_op jit(solution)/shard_map/ppermute | solution.py:11
  1145.8 34.4 %collective-permute-start.7 = (bf16[128,1152]{1,0:T(8,128)(2,1)S(1)}, bf16[128,1152]{1,0:T(8,128)(2,1)S(1)}, u32[]{:S(2)}, u32[]{:S(2)}) collective-permute-start(bf16[128,1152]{1,0:T(8,128)(2,1)S(1)} %collective-permute-done.6), channel_id=1, source_target_pairs={{0,1},{1,2},{2,3},{3,4},{4,5},{5,6},{6,7},{7,8},{8,9},{9,10},{10,1... | collective-permute-start | bytes 884744 | tf_op jit(solution)/shard_map/ppermute | solution.py:11
  1153.6 32.9 %collective-permute-start.14 = (f32[128,1152]{1,0:T(8,128)S(1)}, f32[128,1152]{1,0:T(8,128)S(1)}, u32[]{:S(2)}, u32[]{:S(2)}) collective-permute-start(f32[128,1152]{1,0:T(8,128)S(1)} %add.232), channel_id=1, source_target_pairs={{0,1},{1,2},{2,3},{3,4},{4,5},{5,6},{6,7},{7,8},{8,9},{9,10},{10,1... | collective-permute-start | bytes 1769480 | tf_op jit(solution)/shard_map/ppermute | solution.py:11
  1180.2 33.0 %collective-permute-start.8 = (bf16[128,1152]{1,0:T(8,128)(2,1)S(1)}, bf16[128,1152]{1,0:T(8,128)(2,1)S(1)}, u32[]{:S(2)}, u32[]{:S(2)}) collective-permute-start(bf16[128,1152]{1,0:T(8,128)(2,1)S(1)} %collective-permute-done.7), channel_id=1, source_target_pairs={{0,1},{1,2},{2,3},{3,4},{4,5},{5,6},{6,7},{7,8},{8,9},{9,10},{10,1... | collective-permute-start | bytes 884744 | tf_op jit(solution)/shard_map/ppermute | solution.py:11
  1186.5 32.9 %collective-permute-start.15 = (f32[128,1152]{1,0:T(8,128)S(1)}, f32[128,1152]{1,0:T(8,128)S(1)}, u32[]{:S(2)}, u32[]{:S(2)}) collective-permute-start(f32[128,1152]{1,0:T(8,128)S(1)} %add.233), channel_id=1, source_target_pairs={{0,1},{1,2},{2,3},{3,4},{4,5},{5,6},{6,7},{7,8},{8,9},{9,10},{10,1... | collective-permute-start | bytes 1769480 | tf_op jit(solution)/shard_map/ppermute | solution.py:11
  1219.5 32.8 %collective-permute-start.16 = (f32[128,1152]{1,0:T(8,128)S(1)}, f32[128,1152]{1,0:T(8,128)S(1)}, u32[]{:S(2)}, u32[]{:S(2)}) collective-permute-start(f32[128,1152]{1,0:T(8,128)S(1)} %add.234), channel_id=1, source_target_pairs={{0,1},{1,2},{2,3},{3,4},{4,5},{5,6},{6,7},{7,8},{8,9},{9,10},{10,1... | collective-permute-start | bytes 1769480 | tf_op jit(solution)/shard_map/ppermute | solution.py:11
  1252.5 8.6 collective-permute-start.17
where the time goes:
time: 1260 us
  waiting for transfers between devices  1180 us (94%)
  starting transfers between devices  66.5 us (5%)
    ppermute x18, waiting for transfers between devices, passed_along(): lax.ppermute(x, axis, [(i, (i + by) % devices) for i in range(devices)])  1180 us
    ppermute x18, starting transfers between devices, passed_along(): lax.ppermute(x, axis, [(i, (i + by) % devices) for i in range(devices)])  66.5 us
  transfers between devices with their start and end apart: 18, of which 17 were waited for; matrix products, arithmetic and copies ran while one was open for 1% of the time, Pallas kernels for 0%

commit v1 on v0

v1 whole, which is shorter than its diff:
```python
import jax
import jax.numpy as jnp
from jax import lax
from jax.experimental import pallas as pl
from jax.experimental.pallas import tpu as pltpu
from jax.sharding import PartitionSpec as P

MESH = pl.DeviceIdType.MESH
F32 = jnp.float32
BF16 = jnp.bfloat16

ROWS = 128
WIDTH = 1152
BLOCKS = 9
NZ = 32
CHUNKS = 4
CH = ROWS // CHUNKS

OWN, SIB, PREV, NEXT, EDGE = range(5)


def kernel(
    img_ref, txt_ref, ls_ref, bias_ref,
    loss_ref, gimg_ref, gtxt_ref,
    early, ring, late_r, late_y, acc, loss_acc,
    ring_s, ring_r, next_s, next_r, prev_s, prev_r, sib_s, sib_r,
    fy_s, fy_r, rs_s, rs_r, ys_s, ys_r,
):
    blk, grp = lax.axis_index("blk"), lax.axis_index("grp")
    zhi, core = grp // 2, grp % 2
    zlo, xy = blk // 16, blk % 16
    z = zhi * 16 + zlo

    def at_z(zz):
        return {"blk": (zz % 16) * 16 + xy, "grp": (zz // 16) * 2 + core}

    up, down = at_z((z + 1) % NZ), at_z((z + NZ - 1) % NZ)
    side = 1 - 2 * zhi
    after = {"blk": (blk + side + 256) % 256, "grp": grp}
    before = {"blk": (blk - side + 256) % 256, "grp": grp}
    sibling = {"blk": blk, "grp": grp + 1 - 2 * core}
    role = core + zhi - 2 * core * zhi

    barrier = pltpu.get_barrier_semaphore()
    for dev in (up, down, after, before, sibling):
        pl.semaphore_signal(barrier, inc=1, device_id=dev, device_id_type=MESH)

    for src, i in ((img_ref, 0), (txt_ref, 1)):
        for c in range(CHUNKS):
            r = pl.ds(c * CH, CH)
            x = src[r, :]
            inv = lax.rsqrt(jnp.sum(x * x, axis=1, keepdims=True) + 1e-06)
            early[OWN, i, r, :] = (x * inv).astype(BF16)
    acc[...] = jnp.zeros_like(acc)
    loss_acc[...] = jnp.zeros_like(loss_acc)
    scale = jnp.exp(jnp.full((1, 128), ls_ref[0], F32))
    offset = bias_ref[0]

    pl.semaphore_wait(barrier, 5)

    def remote(src, dst, ss, rs, dev):
        return pltpu.make_async_remote_copy(
            src_ref=src, dst_ref=dst, send_sem=ss, recv_sem=rs, device_id=dev, device_id_type=MESH
        )

    def rows(j):
        return pl.ds(j * CH, CH)

    def hop(h, d, j, first=False, last=False):
        if first:
            src = early.at[OWN if j < CHUNKS // 2 else NEXT, d, rows(j)]
        else:
            src = ring.at[h - 1, d, rows(j)]
        dst = late_r.at[d, rows(j)] if last else ring.at[h, d, rows(j)]
        return remote(src, dst, ring_s.at[h, d, j], ring_r.at[h, d, j], up if d == 0 else down)

    def to_before(d, j):
        return remote(
            early.at[OWN, d, rows(j)], early.at[NEXT, d, rows(j)], next_s.at[d, j], next_r.at[d, j], before
        )

    def to_after(d):
        return remote(early.at[OWN, d], early.at[PREV, d], prev_s.at[d], prev_r.at[d], after)

    own_to_sib = remote(early.at[OWN], early.at[SIB], sib_s.at[0], sib_r.at[0], sibling)
    edge_to_sib = remote(early.at[NEXT - role], early.at[EDGE], sib_s.at[1], sib_r.at[1], sibling)

    for j in range(CHUNKS // 2):
        for d in range(2):
            hop(0, d, j, first=True).start()
            to_before(d, j + CHUNKS // 2).start()
    own_to_sib.start()
    for d in range(2):
        to_after(d).start()
        for j in range(CHUNKS // 2):
            to_before(d, j).start()
    for j in range(CHUNKS // 2, CHUNKS):
        for d in range(2):
            to_before(d, j).wait_recv()
            hop(0, d, j, first=True).start()

    def forward(h, last=False):
        for j in range(CHUNKS):
            for d in range(2):
                hop(h - 1, d, j, first=True).wait_recv()
                hop(h, d, j, last=last).start()

    def unit(i, y, diagonal=None):
        s = lax.dot_general(
            early[OWN, i], y, (((1,), (1,)), ((), ())), preferred_element_type=F32
        )
        u = scale * s + offset
        if diagonal is not None:
            same = lax.broadcasted_iota(jnp.int32, u.shape, 0) == lax.broadcasted_iota(jnp.int32, u.shape, 1)
            flip = jnp.where(same, 1.0 - 2.0 * diagonal, 1.0)
            u = u * flip
        e = jnp.exp(-jnp.abs(u))
        c = scale * (jnp.where(u >= 0, 1.0, e) / (1.0 + e))
        if diagonal is not None:
            c = c * flip
        acc[i] += jnp.dot(c.astype(BF16), y, preferred_element_type=F32)
        if i == 0:
            loss_acc[...] += jnp.maximum(u, 0.0) + jnp.log1p(e)

    def plain(h, _):
        forward(h)
        return _

    lax.fori_loop(1, 6, plain, 0)

    own_to_sib.wait_recv()
    for d in range(2):
        to_after(d).wait_recv()
        for j in range(CHUNKS // 2):
            to_before(d, j).wait_recv()
    edge_to_sib.start()

    def with_unit(p, _):
        diagonal = jnp.where(p == 0, 1.0, 0.0).astype(F32)
        forward(6 + 2 * p)
        unit(0, early[p, 1], diagonal)
        forward(7 + 2 * p)
        unit(1, early[p, 0], diagonal)
        return _

    lax.fori_loop(0, 4, with_unit, 0)
    edge_to_sib.wait_recv()
    forward(14)
    unit(0, early[EDGE, 1])
    forward(15, last=True)
    unit(1, early[EDGE, 0])

    def fwd_y(d, j):
        return remote(
            late_r.at[d, rows(j)], late_y.at[d, rows(j)], fy_s.at[d, j], fy_r.at[d, j],
            after if j < CHUNKS // 2 else before,
        )

    def fwd_rs(d, j):
        return remote(
            late_r.at[d, rows(j)], late_r.at[d, rows(CHUNKS + j)], rs_s.at[d, j], rs_r.at[d, j], sibling
        )

    def fwd_ys(d, j):
        return remote(
            late_y.at[d, rows(j)], late_y.at[d, rows(CHUNKS + j)], ys_s.at[d, j], ys_r.at[d, j], sibling
        )

    chunks = [(d, j) for j in range(CHUNKS) for d in range(2)]
    for d, j in chunks:
        hop(15, d, j, first=True, last=True).wait_recv()
        fwd_y(d, j).start()
        fwd_rs(d, j).start()
    lo, hi = pl.ds(0, ROWS), pl.ds(ROWS, ROWS)
    for i in range(2):
        unit(i, late_r[1 - i, lo])
    for d, j in chunks:
        fwd_y(d, j).wait_recv()
        fwd_ys(d, j).start()
    for d, j in chunks:
        fwd_rs(d, j).wait_recv()
    for i in range(2):
        unit(i, late_r[1 - i, hi])
        unit(i, late_y[1 - i, lo])
    for d, j in chunks:
        fwd_ys(d, j).wait_recv()
    for i in range(2):
        unit(i, late_y[1 - i, hi])

    for src, dst, i in ((img_ref, gimg_ref, 0), (txt_ref, gtxt_ref, 1)):
        for c in range(CHUNKS):
            r = pl.ds(c * CH, CH)
            x = src[r, :]
            g = acc[i, r, :]
            inv = lax.rsqrt(jnp.sum(x * x, axis=1, keepdims=True) + 1e-06)
            x = x * inv
            dst[r, :] = (g - x * jnp.sum(x * g, axis=1, keepdims=True)) * inv
    loss_ref[...] = jnp.sum(loss_acc[...].T, axis=0) / (BLOCKS * ROWS)

    def sent(h, _):
        for d in range(2):
            for j in range(CHUNKS):
                hop(h, d, j, first=True).wait_send()
        return _

    lax.fori_loop(0, 15, sent, 0)
    for d, j in chunks:
        hop(15, d, j, first=True, last=True).wait_send()
        to_before(d, j).wait_send()
        fwd_y(d, j).wait_send()
        fwd_rs(d, j).wait_send()
        fwd_ys(d, j).wait_send()
    for d in range(2):
        to_after(d).wait_send()
    own_to_sib.wait_send()
    edge_to_sib.wait_send()


def on_device(image_emb, text_emb, log_scale, bias):
    vmem, smem = pl.BlockSpec(memory_space=pltpu.VMEM), pl.BlockSpec(memory_space=pltpu.SMEM)
    dma = pltpu.SemaphoreType.DMA
    return pl.pallas_call(
        kernel,
        out_shape=(
            jax.ShapeDtypeStruct((ROWS,), F32),
            jax.ShapeDtypeStruct((ROWS, WIDTH), F32),
            jax.ShapeDtypeStruct((ROWS, WIDTH), F32),
        ),
        in_specs=[vmem, vmem, smem, smem],
        out_specs=(vmem, vmem, vmem),
        scratch_shapes=[
            pltpu.VMEM((5, 2, ROWS, WIDTH), BF16),
            pltpu.VMEM((15, 2, ROWS, WIDTH), BF16),
            pltpu.VMEM((2, 2 * ROWS, WIDTH), BF16),
            pltpu.VMEM((2, 2 * ROWS, WIDTH), BF16),
            pltpu.VMEM((2, ROWS, WIDTH), F32),
            pltpu.VMEM((ROWS, ROWS), F32),
            dma((16, 2, CHUNKS)), dma((16, 2, CHUNKS)),
            dma((2, CHUNKS)), dma((2, CHUNKS)),
            dma((2,)), dma((2,)),
            dma((2,)), dma((2,)),
            dma((2, CHUNKS)), dma((2, CHUNKS)),
            dma((2, CHUNKS)), dma((2, CHUNKS)),
            dma((2, CHUNKS)), dma((2, CHUNKS)),
        ],
        compiler_params=pltpu.CompilerParams(
            collective_id=0, has_side_effects=True, vmem_limit_bytes=40 * 2**20
        ),
    )(image_emb, text_emb, log_scale, bias)


def solution(mesh):
    in_specs = (P(("blk", "grp"), None), P(("blk", "grp"), None), P(), P())
    out_specs = (P(("blk", "grp")), P(("blk", "grp"), None), P(("blk", "grp"), None))
    return jax.shard_map(
        on_device, mesh=mesh, in_specs=in_specs, out_specs=out_specs, check_vma=False
    )
```

time: 1260 us -> 178 us (0.14)
  the two profiles are of different devices: /device:TPU:32 before, /device:TPU:1 now
where the time goes in v1:
time: 178 us
  Pallas kernels  172 us (97%)
  local copies, waits for them, and re-layouts  4.26 us (2%)
  between operations  1.94 us (1%)
    pallas_call x1, Pallas kernels, on_device(): pl.pallas_call(kernel, out_shape=(jax.ShapeDtypeStruct((ROWS,), F32), jax...  172 us
    unnamed x7, local copies, waits for them, and re-layouts  4.26 us

profile of v1, /device:TPU:1, one launch (start us, length us, event | category | flops | bytes accessed | tf_op | source)
XLA Modules:
  0.0 177.9 jit_solution(8039625976372839744)
XLA Ops:
  1.9 0.0 copy-start
  1.9 1.1 copy-done
  3.0 0.0 copy-start.1
  3.0 1.1 copy-done.1
  4.1 171.7 %shard_map.67 = (f32[128]{0:T(128)S(1)}, f32[128,1152]{1,0:T(8,128)S(1)}, f32[128,1152]{1,0:T(8,128)S(1)}) custom-call(f32[128,1152]{1,0:T(8,128)S(1)} %copy-done, f32[128,1152]{1,0:T(8,128)S(1)} %copy-done.1, f32[1]{0:T(128)S(6)} %copy.10.ls_ref, f32[1]{0:T(128)S(6)} %copy.11.bias_ref), custom_call_target="tpu_custom_call" | custom-call | tf_op jit(solution)/shard_map/pallas_call | solution.py:222
  175.8 0.5 copy.12
  176.3 0.8 copy.13
  177.1 0.8 copy.14
Async XLA Ops:
  1.9 1.1 copy-start
  3.0 1.1 copy-start.1

commit v2 on v1

--- a/solution.py
+++ b/solution.py
@@ -22,9 +22,10 @@
 def kernel(
     img_ref, txt_ref, ls_ref, bias_ref,
     loss_ref, gimg_ref, gtxt_ref,
-    early, ring, late_r, late_y, acc, loss_acc,
-    ring_s, ring_r, next_s, next_r, prev_s, prev_r, sib_s, sib_r,
+    emb, early, ring, late_r, late_y, acc, loss_acc, relay,
+    in_sem, ring_s, ring_r, next_s, next_r, prev_s, prev_r, sib_s, sib_r,
     fy_s, fy_r, rs_s, rs_r, ys_s, ys_r,
+    scat_s, scat_r, wrap_s, wrap_r, own_s,
 ):
     blk, grp = lax.axis_index("blk"), lax.axis_index("grp")
     zhi, core = grp // 2, grp % 2
@@ -41,14 +42,54 @@
     sibling = {"blk": blk, "grp": grp + 1 - 2 * core}
     role = core + zhi - 2 * core * zhi
 
+    at_lo, at_hi = xy == 0, xy == 15
+    wrap_next = xy == 15 * (1 - zhi)
+    wrap_prev = xy == 15 * zhi
+    ends = (15, 0)
+    plane = zlo * 16
+    beyond = ((plane + 16) % 256, (plane + 255) % 256)
+    planes = ((plane + 240) % 256, (plane + 16) % 256)
+
+    def dev_at(b):
+        return {"blk": b, "grp": grp}
+
+    half = ROWS // 2
+    loads = []
+    for h in range(2):
+        for src, i in ((img_ref, 0), (txt_ref, 1)):
+            r = pl.ds(h * half, half)
+            copy = pltpu.make_async_copy(src.at[r], emb.at[i, r], in_sem.at[i, h])
+            copy.start()
+            loads.append((copy, i, h))
+
     barrier = pltpu.get_barrier_semaphore()
+
+    def greet(dev):
+        pl.semaphore_signal(barrier, inc=1, device_id=dev, device_id_type=MESH)
+
     for dev in (up, down, after, before, sibling):
-        pl.semaphore_signal(barrier, inc=1, device_id=dev, device_id_type=MESH)
-
-    for src, i in ((img_ref, 0), (txt_ref, 1)):
-        for c in range(CHUNKS):
-            r = pl.ds(c * CH, CH)
-            x = src[r, :]
+        greet(dev)
+    count = 7 + 14 * (xy // 15) + 14 * ((15 - xy) // 15)
+    for k in range(2):
+        is_end = xy == ends[k]
+
+        @pl.when(jnp.logical_not(is_end))
+        def _():
+            greet(dev_at(plane + ends[k]))
+
+        @pl.when(xy == ends[1 - k])
+        def _():
+            def one(c, _):
+                greet(dev_at(planes[k] + c + k))
+                return _
+
+            lax.fori_loop(0, 15, one, 0)
+
+    for copy, i, h in loads:
+        copy.wait()
+        for c in range(2):
+            r = pl.ds(h * half + c * CH, CH)
+            x = emb[i, r, :]
             inv = lax.rsqrt(jnp.sum(x * x, axis=1, keepdims=True) + 1e-06)
             early[OWN, i, r, :] = (x * inv).astype(BF16)
     acc[...] = jnp.zeros_like(acc)
@@ -56,7 +97,7 @@
     scale = jnp.exp(jnp.full((1, 128), ls_ref[0], F32))
     offset = bias_ref[0]
 
-    pl.semaphore_wait(barrier, 5)
+    pl.semaphore_wait(barrier, count)
 
     def remote(src, dst, ss, rs, dev):
         return pltpu.make_async_remote_copy(
@@ -85,25 +126,92 @@
     own_to_sib = remote(early.at[OWN], early.at[SIB], sib_s.at[0], sib_r.at[0], sibling)
     edge_to_sib = remote(early.at[NEXT - role], early.at[EDGE], sib_s.at[1], sib_r.at[1], sibling)
 
+    def unit_of(slot, u):
+        return early.at[slot, u // 8, pl.ds(pl.multiple_of((u % 8) * 16, 16), 16)]
+
+    def scatter(k, c):
+        return remote(unit_of(OWN, c), relay.at[k], scat_s.at[k, c], scat_r.at[k], dev_at(plane + c))
+
+    def relayed(k, u):
+        slot = 2 + zhi if k == 0 else 3 - zhi
+        return remote(relay.at[k], unit_of(slot, u), wrap_s.at[k], wrap_r.at[k, u], dev_at(beyond[k]))
+
+    def straight(k):
+        slot = 2 + zhi if k == 0 else 3 - zhi
+        return remote(
+            unit_of(OWN, ends[k]), unit_of(slot, ends[k]), own_s.at[k], wrap_r.at[k, ends[k]], dev_at(beyond[k])
+        )
+
+    def wait_units(k, rows_from):
+        def one(v, _):
+            relayed(k, (v // 4) * 8 + rows_from + v % 4).wait_recv()
+            return _
+
+        lax.fori_loop(0, 8, one, 0)
+
+    def on_side(wrapped, fn):
+        for k in range(2):
+            @pl.when(wrapped & (at_lo if k == 0 else at_hi))
+            def _():
+                fn(k)
+
     for j in range(CHUNKS // 2):
         for d in range(2):
             hop(0, d, j, first=True).start()
-            to_before(d, j + CHUNKS // 2).start()
+    for k in range(2):
+        @pl.when(xy == ends[k])
+        def _():
+            straight(k).start()
+
+            def one(c, _):
+                scatter(k, c + k).start()
+                return _
+
+            lax.fori_loop(0, 15, one, 0)
+
+    @pl.when(jnp.logical_not(wrap_prev))
+    def _():
+        for j in range(CHUNKS // 2, CHUNKS):
+            for d in range(2):
+                to_before(d, j).start()
+
+    @pl.when(jnp.logical_not(wrap_next))
+    def _():
+        for d in range(2):
+            to_after(d).start()
+
+    @pl.when(jnp.logical_not(wrap_prev))
+    def _():
+        for j in range(CHUNKS // 2):
+            for d in range(2):
+                to_before(d, j).start()
+
     own_to_sib.start()
-    for d in range(2):
-        to_after(d).start()
-        for j in range(CHUNKS // 2):
-            to_before(d, j).start()
-    for j in range(CHUNKS // 2, CHUNKS):
-        for d in range(2):
-            to_before(d, j).wait_recv()
-            hop(0, d, j, first=True).start()
-
-    def forward(h, last=False):
-        for j in range(CHUNKS):
+    for k in range(2):
+        @pl.when(xy != ends[k])
+        def _():
+            scatter(k, xy).wait_recv()
+            relayed(k, xy).start()
+
+    def forward(h, parts=(0, 2, 1, 3), last=False):
+        for j in parts:
             for d in range(2):
                 hop(h - 1, d, j, first=True).wait_recv()
                 hop(h, d, j, last=last).start()
+
+    FRONT, BACK = (0, 1), (2, 3)
+    forward(1, FRONT)
+
+    @pl.when(jnp.logical_not(wrap_next))
+    def _():
+        for j in BACK:
+            for d in range(2):
+                to_before(d, j).wait_recv()
+
+    on_side(wrap_next, lambda k: wait_units(k, 4))
+    for j in BACK:
+        for d in range(2):
+            hop(0, d, j, first=True).start()
 
     def unit(i, y, diagonal=None):
         s = lax.dot_general(
@@ -122,17 +230,34 @@
         if i == 0:
             loss_acc[...] += jnp.maximum(u, 0.0) + jnp.log1p(e)
 
-    def plain(h, _):
-        forward(h)
+    def skewed(h, _):
+        forward(h, FRONT)
+        forward(h - 1, BACK)
         return _
 
-    lax.fori_loop(1, 6, plain, 0)
+    lax.fori_loop(2, 6, skewed, 0)
+    forward(5, BACK)
 
     own_to_sib.wait_recv()
-    for d in range(2):
-        to_after(d).wait_recv()
-        for j in range(CHUNKS // 2):
-            to_before(d, j).wait_recv()
+
+    @pl.when(jnp.logical_not(wrap_next))
+    def _():
+        for d in range(2):
+            for j in FRONT:
+                to_before(d, j).wait_recv()
+
+    @pl.when(jnp.logical_not(wrap_prev))
+    def _():
+        for d in range(2):
+            to_after(d).wait_recv()
+
+    on_side(wrap_next, lambda k: wait_units(k, 0))
+
+    def all_units(k):
+        wait_units(k, 0)
+        wait_units(k, 4)
+
+    on_side(wrap_prev, all_units)
     edge_to_sib.start()
 
     def with_unit(p, _):
@@ -166,7 +291,7 @@
             late_y.at[d, rows(j)], late_y.at[d, rows(CHUNKS + j)], ys_s.at[d, j], ys_r.at[d, j], sibling
         )
 
-    chunks = [(d, j) for j in range(CHUNKS) for d in range(2)]
+    chunks = [(d, j) for j in (0, 2, 1, 3) for d in range(2)]
     for d, j in chunks:
         hop(15, d, j, first=True, last=True).wait_recv()
         fwd_y(d, j).start()
@@ -187,10 +312,10 @@
     for i in range(2):
         unit(i, late_y[1 - i, hi])
 
-    for src, dst, i in ((img_ref, gimg_ref, 0), (txt_ref, gtxt_ref, 1)):
+    for dst, i in ((gimg_ref, 0), (gtxt_ref, 1)):
         for c in range(CHUNKS):
             r = pl.ds(c * CH, CH)
-            x = src[r, :]
+            x = emb[i, r, :]
             g = acc[i, r, :]
             inv = lax.rsqrt(jnp.sum(x * x, axis=1, keepdims=True) + 1e-06)
             x = x * inv
@@ -206,12 +331,35 @@
     lax.fori_loop(0, 15, sent, 0)
     for d, j in chunks:
         hop(15, d, j, first=True, last=True).wait_send()
-        to_before(d, j).wait_send()
         fwd_y(d, j).wait_send()
         fwd_rs(d, j).wait_send()
         fwd_ys(d, j).wait_send()
-    for d in range(2):
-        to_after(d).wait_send()
+
+    @pl.when(jnp.logical_not(wrap_prev))
+    def _():
+        for d, j in chunks:
+            to_before(d, j).wait_send()
+
+    @pl.when(jnp.logical_not(wrap_next))
+    def _():
+        for d in range(2):
+            to_after(d).wait_send()
+
+    for k in range(2):
+        @pl.when(xy == ends[k])
+        def _():
+            straight(k).wait_send()
+
+            def one(c, _):
+                scatter(k, c + k).wait_send()
+                return _
+
+            lax.fori_loop(0, 15, one, 0)
+
+        @pl.when(xy != ends[k])
+        def _():
+            relayed(k, xy).wait_send()
+
     own_to_sib.wait_send()
     edge_to_sib.wait_send()
 
@@ -226,15 +374,18 @@
             jax.ShapeDtypeStruct((ROWS, WIDTH), F32),
             jax.ShapeDtypeStruct((ROWS, WIDTH), F32),
         ),
-        in_specs=[vmem, vmem, smem, smem],
+        in_specs=[pl.BlockSpec(memory_space=pl.ANY)] * 2 + [smem, smem],
         out_specs=(vmem, vmem, vmem),
         scratch_shapes=[
+            pltpu.VMEM((2, ROWS, WIDTH), F32),
             pltpu.VMEM((5, 2, ROWS, WIDTH), BF16),
             pltpu.VMEM((15, 2, ROWS, WIDTH), BF16),
             pltpu.VMEM((2, 2 * ROWS, WIDTH), BF16),
             pltpu.VMEM((2, 2 * ROWS, WIDTH), BF16),
             pltpu.VMEM((2, ROWS, WIDTH), F32),
             pltpu.VMEM((ROWS, ROWS), F32),
+            pltpu.VMEM((2, 16, WIDTH), BF16),
+            dma((2, 2)),
             dma((16, 2, CHUNKS)), dma((16, 2, CHUNKS)),
             dma((2, CHUNKS)), dma((2, CHUNKS)),
             dma((2,)), dma((2,)),
@@ -242,6 +393,7 @@
             dma((2, CHUNKS)), dma((2, CHUNKS)),
             dma((2, CHUNKS)), dma((2, CHUNKS)),
             dma((2, CHUNKS)), dma((2, CHUNKS)),
+            dma((2, 16)), dma((2,)), dma((2,)), dma((2, 16)), dma((2,)),
         ],
         compiler_params=pltpu.CompilerParams(
             collective_id=0, has_side_effects=True, vmem_limit_bytes=40 * 2**20

time: 178 us -> 174 us (0.978)
  Pallas kernels: 172 us -> 168 us
    pallas_call x1, Pallas kernels: 172 us -> 168 us  [on_device(): pl.pallas_call(kernel, out_shape=(jax.ShapeDtypeStruct((ROWS,), F32), jax...]
where the time goes in v2:
time: 174 us
  Pallas kernels  168 us (97%)
  local copies, waits for them, and re-layouts  4.26 us (2%)
  between operations  1.94 us (1%)
    pallas_call x1, Pallas kernels, on_device(): pl.pallas_call(kernel, out_shape=(jax.ShapeDtypeStruct((ROWS,), F32), jax...  168 us
    unnamed x7, local copies, waits for them, and re-layouts  4.26 us

profile of v2, /device:TPU:1, one launch (start us, length us, event | category | flops | bytes accessed | tf_op | source)
XLA Modules:
  0.0 173.8 jit_solution(12236972033528409837)
XLA Ops:
  1.9 0.0 copy-start
  1.9 1.1 copy-done
  3.0 0.0 copy-start.1
  3.0 1.1 copy-done.1
  4.1 167.6 %shard_map.67 = (f32[128]{0:T(128)S(1)}, f32[128,1152]{1,0:T(8,128)S(1)}, f32[128,1152]{1,0:T(8,128)S(1)}) custom-call(f32[128,1152]{1,0:T(8,128)S(1)} %copy-done, f32[128,1152]{1,0:T(8,128)S(1)} %copy-done.1, f32[1]{0:T(128)S(6)} %copy.10.ls_ref, f32[1]{0:T(128)S(6)} %copy.11.bias_ref), custom_call_target="tpu_custom_call" | custom-call | tf_op jit(solution)/shard_map/pallas_call | solution.py:370
  171.7 0.5 copy.12
  172.2 0.8 copy.13
  173.0 0.8 copy.14
Async XLA Ops:
  1.9 1.1 copy-start
  3.0 1.1 copy-start.1

commit v3 on v2

--- a/solution.py
+++ b/solution.py
@@ -16,7 +16,7 @@
 CHUNKS = 4
 CH = ROWS // CHUNKS
 
-OWN, SIB, PREV, NEXT, EDGE = range(5)
+OWN, SIB, PREV, NEXT, EDGE, XTRA = range(6)
 
 
 def kernel(
@@ -25,7 +25,7 @@
     emb, early, ring, late_r, late_y, acc, loss_acc, relay,
     in_sem, ring_s, ring_r, next_s, next_r, prev_s, prev_r, sib_s, sib_r,
     fy_s, fy_r, rs_s, rs_r, ys_s, ys_r,
-    scat_s, scat_r, wrap_s, wrap_r, own_s,
+    scat_s, scat_r, wrap_s, wrap_r, own_s, xtra_s, xtra_r,
 ):
     blk, grp = lax.axis_index("blk"), lax.axis_index("grp")
     zhi, core = grp // 2, grp % 2
@@ -37,21 +37,24 @@
 
     up, down = at_z((z + 1) % NZ), at_z((z + NZ - 1) % NZ)
     side = 1 - 2 * zhi
-    after = {"blk": (blk + side + 256) % 256, "grp": grp}
-    before = {"blk": (blk - side + 256) % 256, "grp": grp}
+    place = z * 16 + xy
+
+    def at_place(p):
+        return {"blk": p % 256, "grp": (p // 256) * 2 + core}
+
+    after, before = at_place((place + side + 512) % 512), at_place((place - side + 512) % 512)
     sibling = {"blk": blk, "grp": grp + 1 - 2 * core}
     role = core + zhi - 2 * core * zhi
+    inner = ((place + 1) // 256) * (1 - place // 257)
+    outer = (511 - place) // 511 + place // 511
 
     at_lo, at_hi = xy == 0, xy == 15
     wrap_next = xy == 15 * (1 - zhi)
     wrap_prev = xy == 15 * zhi
     ends = (15, 0)
-    plane = zlo * 16
-    beyond = ((plane + 16) % 256, (plane + 255) % 256)
-    planes = ((plane + 240) % 256, (plane + 16) % 256)
-
-    def dev_at(b):
-        return {"blk": b, "grp": grp}
+    plane = z * 16
+    beyond = ((plane + 16) % 512, (plane + 511) % 512)
+    planes = ((plane + 496) % 512, (plane + 16) % 512)
 
     half = ROWS // 2
     loads = []
@@ -75,12 +78,12 @@
 
         @pl.when(jnp.logical_not(is_end))
         def _():
-            greet(dev_at(plane + ends[k]))
+            greet(at_place(plane + ends[k]))
 
         @pl.when(xy == ends[1 - k])
         def _():
             def one(c, _):
-                greet(dev_at(planes[k] + c + k))
+                greet(at_place(planes[k] + c + k))
                 return _
 
             lax.fori_loop(0, 15, one, 0)
@@ -125,26 +128,28 @@
 
     own_to_sib = remote(early.at[OWN], early.at[SIB], sib_s.at[0], sib_r.at[0], sibling)
     edge_to_sib = remote(early.at[NEXT - role], early.at[EDGE], sib_s.at[1], sib_r.at[1], sibling)
+    xtra_to_sib = remote(early.at[XTRA], early.at[EDGE], sib_s.at[1], sib_r.at[1], sibling)
 
     def unit_of(slot, u):
         return early.at[slot, u // 8, pl.ds(pl.multiple_of((u % 8) * 16, 16), 16)]
 
     def scatter(k, c):
-        return remote(unit_of(OWN, c), relay.at[k], scat_s.at[k, c], scat_r.at[k], dev_at(plane + c))
-
-    def relayed(k, u):
-        slot = 2 + zhi if k == 0 else 3 - zhi
-        return remote(relay.at[k], unit_of(slot, u), wrap_s.at[k], wrap_r.at[k, u], dev_at(beyond[k]))
+        return remote(unit_of(OWN, c), relay.at[k], scat_s.at[k, c], scat_r.at[k], at_place(plane + c))
+
+    here = (2 + zhi, 3 - zhi)
+    there = (2 + ((z + 1) % NZ) // 16, 3 - ((z + NZ - 1) % NZ) // 16)
+
+    def relayed(k, u, slot):
+        return remote(relay.at[k], unit_of(slot, u), wrap_s.at[k], wrap_r.at[k, u], at_place(beyond[k]))
 
     def straight(k):
-        slot = 2 + zhi if k == 0 else 3 - zhi
         return remote(
-            unit_of(OWN, ends[k]), unit_of(slot, ends[k]), own_s.at[k], wrap_r.at[k, ends[k]], dev_at(beyond[k])
+            unit_of(OWN, ends[k]), unit_of(there[k], ends[k]), own_s.at[k], wrap_r.at[k, ends[k]], at_place(beyond[k])
         )
 
     def wait_units(k, rows_from):
         def one(v, _):
-            relayed(k, (v // 4) * 8 + rows_from + v % 4).wait_recv()
+            relayed(k, (v // 4) * 8 + rows_from + v % 4, here[k]).wait_recv()
             return _
 
         lax.fori_loop(0, 8, one, 0)
@@ -191,7 +196,7 @@
         @pl.when(xy != ends[k])
         def _():
             scatter(k, xy).wait_recv()
-            relayed(k, xy).start()
+            relayed(k, xy, there[k]).start()
 
     def forward(h, parts=(0, 2, 1, 3), last=False):
         for j in parts:
@@ -199,6 +204,23 @@
                 hop(h - 1, d, j, first=True).wait_recv()
                 hop(h, d, j, last=last).start()
 
+    def xtra(d, j, src=XTRA, src_row=0):
+        return remote(
+            early.at[src, d, pl.ds((j + src_row) * CH, CH)], early.at[XTRA, d, rows(j)],
+            xtra_s.at[d, j], xtra_r.at[d, j], up if d == 0 else down,
+        )
+
+    in_end = at_lo | at_hi
+    origin = 31 * (xy // 15)
+
+    def forward_xtra(h):
+        for d in range(2):
+            @pl.when(in_end & ((z + NZ - h if d == 0 else z + h) % NZ == origin))
+            def _():
+                for j in range(CHUNKS):
+                    xtra(d, j).wait_recv()
+                    xtra(d, j).start()
+
     FRONT, BACK = (0, 1), (2, 3)
     forward(1, FRONT)
 
@@ -212,6 +234,18 @@
     for j in BACK:
         for d in range(2):
             hop(0, d, j, first=True).start()
+
+    @pl.when(outer == 1)
+    def _():
+        for k in range(2):
+            @pl.when(at_lo if k == 0 else at_hi)
+            def _():
+                wait_units(k, 0)
+                wait_units(k, 4)
+
+        for j in range(CHUNKS):
+            for d in range(2):
+                xtra(d, j, PREV if j < CHUNKS // 2 else OWN, CHUNKS // 2 if j < CHUNKS // 2 else 0).start()
 
     def unit(i, y, diagonal=None):
         s = lax.dot_general(
@@ -233,10 +267,12 @@
     def skewed(h, _):
         forward(h, FRONT)
         forward(h - 1, BACK)
+        forward_xtra(h - 1)
         return _
 
     lax.fori_loop(2, 6, skewed, 0)
     forward(5, BACK)
+    forward_xtra(5)
 
     own_to_sib.wait_recv()
 
@@ -257,56 +293,114 @@
         wait_units(k, 0)
         wait_units(k, 4)
 
-    on_side(wrap_prev, all_units)
-    edge_to_sib.start()
-
-    def with_unit(p, _):
+    on_side(wrap_prev & (outer == 0), all_units)
+
+    @pl.when(inner * (1 - role) == 0)
+    def _():
+        edge_to_sib.start()
+
+    def with_unit(p, carry):
         diagonal = jnp.where(p == 0, 1.0, 0.0).astype(F32)
-        forward(6 + 2 * p)
-        unit(0, early[p, 1], diagonal)
-        forward(7 + 2 * p)
-        unit(1, early[p, 0], diagonal)
-        return _
+        used = inner * (p // 3) == 0
+        for i in range(2):
+            forward(6 + 2 * p + i)
+            forward_xtra(6 + 2 * p + i)
+
+            @pl.when(used)
+            def _():
+                unit(i, early[p, 1 - i], diagonal)
+        return carry
 
     lax.fori_loop(0, 4, with_unit, 0)
-    edge_to_sib.wait_recv()
-    forward(14)
-    unit(0, early[EDGE, 1])
-    forward(15, last=True)
-    unit(1, early[EDGE, 0])
+    edge_early = inner * role == 0
+
+    @pl.when(edge_early)
+    def _():
+        edge_to_sib.wait_recv()
+
+    for i in range(2):
+        forward(14 + i, last=i == 1)
+        forward_xtra(14 + i)
+
+        @pl.when(edge_early)
+        def _():
+            unit(i, early[EDGE, 1 - i])
+
+    def part_rows(j):
+        return pl.ds(pl.multiple_of(j * CH, CH), CH)
 
     def fwd_y(d, j):
+        if j < CHUNKS // 2:
+            src, dst, dev = j, j + 2 * inner, after
+        else:
+            src, dst, dev = j - 2 * outer, j - 2 * outer, before
         return remote(
-            late_r.at[d, rows(j)], late_y.at[d, rows(j)], fy_s.at[d, j], fy_r.at[d, j],
-            after if j < CHUNKS // 2 else before,
+            late_r.at[d, part_rows(src)], late_y.at[d, part_rows(dst)], fy_s.at[d, j], fy_r.at[d, dst], dev
         )
 
-    def fwd_rs(d, j):
-        return remote(
-            late_r.at[d, rows(j)], late_r.at[d, rows(CHUNKS + j)], rs_s.at[d, j], rs_r.at[d, j], sibling
-        )
-
-    def fwd_ys(d, j):
-        return remote(
-            late_y.at[d, rows(j)], late_y.at[d, rows(CHUNKS + j)], ys_s.at[d, j], ys_r.at[d, j], sibling
-        )
-
+    def got_y(d, j):
+        return remote(late_r.at[d, rows(j)], late_y.at[d, rows(j)], fy_s.at[d, j], fy_r.at[d, j], after)
+
+    def fwd_rs(d, j, other=None):
+        src = late_r.at[d, rows(j)] if other is None else early.at[other, d, rows(j)]
+        return remote(src, late_r.at[d, rows(CHUNKS + j)], rs_s.at[d, j], rs_r.at[d, j], sibling)
+
+    def fwd_ys(d, j, other=None):
+        src = late_y.at[d, rows(j)] if other is None else early.at[other, d, rows(j)]
+        return remote(src, late_y.at[d, rows(CHUNKS + j)], ys_s.at[d, j], ys_r.at[d, j], sibling)
+
+    def either(copy, other, which):
+        @pl.when(which)
+        def _():
+            copy(other).start()
+
+        @pl.when(jnp.logical_not(which))
+        def _():
+            copy(None).start()
+
+    outer_first, inner_second = outer * (1 - role) == 1, inner * role == 1
     chunks = [(d, j) for j in (0, 2, 1, 3) for d in range(2)]
     for d, j in chunks:
         hop(15, d, j, first=True, last=True).wait_recv()
         fwd_y(d, j).start()
-        fwd_rs(d, j).start()
+        if j < CHUNKS // 2:
+            fwd_rs(d, j).start()
+        else:
+            either(lambda other: fwd_rs(d, j, other), PREV, outer_first)
+
+    @pl.when(inner == 1)
+    def _():
+        for d, j in chunks:
+            xtra(d, j).wait_recv()
+
+        @pl.when(role == 0)
+        def _():
+            xtra_to_sib.start()
+
+        for i in range(2):
+            unit(i, early[XTRA, 1 - i])
+
     lo, hi = pl.ds(0, ROWS), pl.ds(ROWS, ROWS)
     for i in range(2):
         unit(i, late_r[1 - i, lo])
     for d, j in chunks:
-        fwd_y(d, j).wait_recv()
-        fwd_ys(d, j).start()
+        got_y(d, j).wait_recv()
+        if j < CHUNKS // 2:
+            either(lambda other: fwd_ys(d, j, other), PREV, outer_first)
+        else:
+            either(lambda other: fwd_ys(d, j, other), XTRA, inner_second)
     for d, j in chunks:
         fwd_rs(d, j).wait_recv()
     for i in range(2):
         unit(i, late_r[1 - i, hi])
         unit(i, late_y[1 - i, lo])
+
+    @pl.when(inner * role == 1)
+    def _():
+        xtra_to_sib.wait_recv()
+        for i in range(2):
+            unit(i, early[EDGE, 1 - i])
+
     for d, j in chunks:
         fwd_ys(d, j).wait_recv()
     for i in range(2):
@@ -358,7 +452,20 @@
 
         @pl.when(xy != ends[k])
         def _():
-            relayed(k, xy).wait_send()
+            relayed(k, xy, there[k]).wait_send()
+
+    @pl.when(outer == 1)
+    def _():
+        for d, j in chunks:
+            xtra(d, j).wait_send()
+
+    for d in range(2):
+        gone = (z + NZ - origin if d == 0 else origin + NZ - z) % NZ
+
+        @pl.when(in_end & (gone >= 1) & (gone <= 15))
+        def _():
+            for j in range(CHUNKS):
+                xtra(d, j).wait_send()
 
     own_to_sib.wait_send()
     edge_to_sib.wait_send()
@@ -378,7 +485,7 @@
         out_specs=(vmem, vmem, vmem),
         scratch_shapes=[
             pltpu.VMEM((2, ROWS, WIDTH), F32),
-            pltpu.VMEM((5, 2, ROWS, WIDTH), BF16),
+            pltpu.VMEM((6, 2, ROWS, WIDTH), BF16),
             pltpu.VMEM((15, 2, ROWS, WIDTH), BF16),
             pltpu.VMEM((2, 2 * ROWS, WIDTH), BF16),
             pltpu.VMEM((2, 2 * ROWS, WIDTH), BF16),
@@ -393,10 +500,10 @@
             dma((2, CHUNKS)), dma((2, CHUNKS)),
             dma((2, CHUNKS)), dma((2, CHUNKS)),
             dma((2, CHUNKS)), dma((2, CHUNKS)),
-            dma((2, 16)), dma((2,)), dma((2,)), dma((2, 16)), dma((2,)),
+            dma((2, 16)), dma((2,)), dma((2,)), dma((2, 16)), dma((2,)), dma((2, CHUNKS)), dma((2, CHUNKS)),
         ],
         compiler_params=pltpu.CompilerParams(
-            collective_id=0, has_side_effects=True, vmem_limit_bytes=40 * 2**20
+            collective_id=0, has_side_effects=True, vmem_limit_bytes=60 * 2**20
         ),
     )(image_emb, text_emb, log_scale, bias)
 

time: 174 us -> 158 us (0.908)
  Pallas kernels: 168 us -> 152 us
    pallas_call x1, Pallas kernels: 168 us -> 152 us  [on_device(): pl.pallas_call(kernel, out_shape=(jax.ShapeDtypeStruct((ROWS,), F32), jax...]
where the time goes in v3:
time: 158 us; the launch traced here: 157 us
  Pallas kernels  152 us (96%)
  local copies, waits for them, and re-layouts  3.92 us (2%)
  between operations  1.94 us (1%)
    pallas_call x1, Pallas kernels, on_device(): pl.pallas_call(kernel, out_shape=(jax.ShapeDtypeStruct((ROWS,), F32), jax...  152 us
    unnamed x7, local copies, waits for them, and re-layouts  3.92 us

profile of v3, /device:TPU:1, one launch (start us, length us, event | category | flops | bytes accessed | tf_op | source)
XLA Modules:
  0.0 157.5 jit_solution(10510085018408990934)
XLA Ops:
  1.9 151.6 %shard_map.67 = (f32[128]{0:T(128)}, f32[128,1152]{1,0:T(8,128)}, f32[128,1152]{1,0:T(8,128)}) custom-call(f32[128,1152]{1,0:T(8,128)} %img_ref.1, f32[128,1152]{1,0:T(8,128)} %txt_ref.1, f32[1]{0:T(128)S(6)} %copy.10.ls_ref, f32[1]{0:T(128)S(6)} %copy.11.bias_ref), custom_call_target="tpu_custom_call" | custom-call | tf_op jit(solution)/shard_map/pallas_call | solution.py:477
  153.6 0.0 copy-start.1
  153.6 0.6 copy-done.1
  154.2 0.5 copy.12
  154.7 0.0 copy-start
  154.7 2.0 %copy.13 = f32[128,1152]{1,0:T(8,128)} copy(f32[128,1152]{1,0:T(8,128)} %get-tuple-element.7) | data formatting | bytes 1179648
  156.7 0.0 copy-done
  156.7 0.8 copy.14
Async XLA Ops:
  153.6 0.6 copy-start.1
  154.7 2.0 %copy-start = (f32[128,1152]{1,0:T(8,128)S(1)}, f32[128,1152]{1,0:T(8,128)}, u32[]{:S(2)}) copy-start(f32[128,1152]{1,0:T(8,128)} %get-tuple-element.8) | copy-start | bytes 1769476

commit v4 on v3

--- a/solution.py
+++ b/solution.py
@@ -22,10 +22,10 @@
 def kernel(
     img_ref, txt_ref, ls_ref, bias_ref,
     loss_ref, gimg_ref, gtxt_ref,
-    emb, early, ring, late_r, late_y, acc, loss_acc, relay,
+    emb, early, ring, late_r, late_y, acc, loss_acc, relay, xbuf,
     in_sem, ring_s, ring_r, next_s, next_r, prev_s, prev_r, sib_s, sib_r,
     fy_s, fy_r, rs_s, rs_r, ys_s, ys_r,
-    scat_s, scat_r, wrap_s, wrap_r, own_s, xtra_s, xtra_r,
+    scat_s, scat_r, wrap_s, wrap_r, own_s, flow_s, flow_r, drop_s, xtra_r,
 ):
     blk, grp = lax.axis_index("blk"), lax.axis_index("grp")
     zhi, core = grp // 2, grp % 2
@@ -47,6 +47,11 @@
     role = core + zhi - 2 * core * zhi
     inner = ((place + 1) // 256) * (1 - place // 257)
     outer = (511 - place) // 511 + place // 511
+    carrier = (xy % 8) // 4
+    mid = ((z + 1) // 16) * (1 - z // 17)
+    itself = inner * (1 - zhi)
+    dropping = carrier * mid * (1 - itself) == 1
+    gone = (z, NZ - 1 - z)
 
     at_lo, at_hi = xy == 0, xy == 15
     wrap_next = xy == 15 * (1 - zhi)
@@ -72,7 +77,7 @@
 
     for dev in (up, down, after, before, sibling):
         greet(dev)
-    count = 7 + 14 * (xy // 15) + 14 * ((15 - xy) // 15)
+    count = 7 + 14 * (xy // 15) + 14 * ((15 - xy) // 15) + carrier * mid * (1 - itself)
     for k in range(2):
         is_end = xy == ends[k]
 
@@ -87,6 +92,14 @@
                 return _
 
             lax.fori_loop(0, 15, one, 0)
+
+    @pl.when(inner == 1)
+    def _():
+        def one(v, _):
+            greet(at_place(plane + (v // 4) * 8 + 4 + v % 4))
+            return _
+
+        lax.fori_loop(0, 7 + zhi, one, 0)
 
     for copy, i, h in loads:
         copy.wait()
@@ -192,11 +205,25 @@
                 to_before(d, j).start()
 
     own_to_sib.start()
+
+    def flow(d, src=None):
+        return remote(
+            xbuf.at[d] if src is None else src, xbuf.at[d], flow_s.at[d], flow_r.at[d], up if d == 0 else down
+        )
+
     for k in range(2):
         @pl.when(xy != ends[k])
         def _():
             scatter(k, xy).wait_recv()
             relayed(k, xy, there[k]).start()
+
+            @pl.when((carrier == 1) & (gone[1 - k] == 0))
+            def _():
+                flow(1 - k, relay.at[k]).start()
+
+    @pl.when(place == 511)
+    def _():
+        flow(1, unit_of(OWN, 15)).start()
 
     def forward(h, parts=(0, 2, 1, 3), last=False):
         for j in parts:
@@ -204,22 +231,22 @@
                 hop(h - 1, d, j, first=True).wait_recv()
                 hop(h, d, j, last=last).start()
 
-    def xtra(d, j, src=XTRA, src_row=0):
+    def forward_xtra(h):
+        for d in range(2):
+            @pl.when((carrier == 1) & (gone[d] == h))
+            def _():
+                flow(d).wait_recv()
+                flow(d).start()
+
+    def xtra_rows(d, v):
+        return pl.ds(pl.multiple_of((d + zhi - 2 * d * zhi) * half + (v % 4) * 16, 16), 16)
+
+    def drop(d, v):
         return remote(
-            early.at[src, d, pl.ds((j + src_row) * CH, CH)], early.at[XTRA, d, rows(j)],
-            xtra_s.at[d, j], xtra_r.at[d, j], up if d == 0 else down,
-        )
-
-    in_end = at_lo | at_hi
-    origin = 31 * (xy // 15)
-
-    def forward_xtra(h):
-        for d in range(2):
-            @pl.when(in_end & ((z + NZ - h if d == 0 else z + h) % NZ == origin))
-            def _():
-                for j in range(CHUNKS):
-                    xtra(d, j).wait_recv()
-                    xtra(d, j).start()
+            xbuf.at[d], early.at[XTRA, v // 4, xtra_rows(d, v)], drop_s.at[d], xtra_r.at[d, v], at_place(z + 240)
+        )
+
+    mine = (xy // 8) * 4 + xy % 4
 
     FRONT, BACK = (0, 1), (2, 3)
     forward(1, FRONT)
@@ -234,18 +261,6 @@
     for j in BACK:
         for d in range(2):
             hop(0, d, j, first=True).start()
-
-    @pl.when(outer == 1)
-    def _():
-        for k in range(2):
-            @pl.when(at_lo if k == 0 else at_hi)
-            def _():
-                wait_units(k, 0)
-                wait_units(k, 4)
-
-        for j in range(CHUNKS):
-            for d in range(2):
-                xtra(d, j, PREV if j < CHUNKS // 2 else OWN, CHUNKS // 2 if j < CHUNKS // 2 else 0).start()
 
     def unit(i, y, diagonal=None):
         s = lax.dot_general(
@@ -293,7 +308,7 @@
         wait_units(k, 0)
         wait_units(k, 4)
 
-    on_side(wrap_prev & (outer == 0), all_units)
+    on_side(wrap_prev, all_units)
 
     @pl.when(inner * (1 - role) == 0)
     def _():
@@ -368,10 +383,29 @@
         else:
             either(lambda other: fwd_rs(d, j, other), PREV, outer_first)
 
+    for d in range(2):
+        @pl.when(carrier * mid == 1)
+        def _():
+            @pl.when(gone[d] == 16)
+            def _():
+                flow(d).wait_recv()
+
+        @pl.when(dropping)
+        def _():
+            drop(d, mine).start()
+
+        @pl.when(itself == 1)
+        def _():
+            early[XTRA, 1, pl.ds(d * half + 48, 16), :] = xbuf[d]
+
     @pl.when(inner == 1)
     def _():
-        for d, j in chunks:
-            xtra(d, j).wait_recv()
+        for d in range(2):
+            def one(v, _):
+                drop(d, v).wait_recv()
+                return _
+
+            lax.fori_loop(0, 7 + zhi, one, 0)
 
         @pl.when(role == 0)
         def _():
@@ -454,18 +488,14 @@
         def _():
             relayed(k, xy, there[k]).wait_send()
 
-    @pl.when(outer == 1)
-    def _():
-        for d, j in chunks:
-            xtra(d, j).wait_send()
-
     for d in range(2):
-        gone = (z + NZ - origin if d == 0 else origin + NZ - z) % NZ
-
-        @pl.when(in_end & (gone >= 1) & (gone <= 15))
-        def _():
-            for j in range(CHUNKS):
-                xtra(d, j).wait_send()
+        @pl.when((carrier == 1) & (gone[d] <= 15))
+        def _():
+            flow(d).wait_send()
+
+        @pl.when(dropping)
+        def _():
+            drop(d, mine).wait_send()
 
     own_to_sib.wait_send()
     edge_to_sib.wait_send()
@@ -492,6 +522,7 @@
             pltpu.VMEM((2, ROWS, WIDTH), F32),
             pltpu.VMEM((ROWS, ROWS), F32),
             pltpu.VMEM((2, 16, WIDTH), BF16),
+            pltpu.VMEM((2, 16, WIDTH), BF16),
             dma((2, 2)),
             dma((16, 2, CHUNKS)), dma((16, 2, CHUNKS)),
             dma((2, CHUNKS)), dma((2, CHUNKS)),
@@ -500,10 +531,11 @@
             dma((2, CHUNKS)), dma((2, CHUNKS)),
             dma((2, CHUNKS)), dma((2, CHUNKS)),
             dma((2, CHUNKS)), dma((2, CHUNKS)),
-            dma((2, 16)), dma((2,)), dma((2,)), dma((2, 16)), dma((2,)), dma((2, CHUNKS)), dma((2, CHUNKS)),
+            dma((2, 16)), dma((2,)), dma((2,)), dma((2, 16)), dma((2,)),
+            dma((2,)), dma((2,)), dma((2,)), dma((2, 8)),
         ],
         compiler_params=pltpu.CompilerParams(
-            collective_id=0, has_side_effects=True, vmem_limit_bytes=60 * 2**20
+            collective_id=0, has_side_effects=True, vmem_limit_bytes=55050240
         ),
     )(image_emb, text_emb, log_scale, bias)
 

time: 158 us -> 149 us (0.943)
  Pallas kernels: 152 us -> 145 us
  local copies, waits for them, and re-layouts: 3.92 us -> 2.14 us
    pallas_call x1, Pallas kernels: 152 us -> 145 us  [on_device(): pl.pallas_call(kernel, out_shape=(jax.ShapeDtypeStruct((ROWS,), F32), jax...]
    unnamed x7 -> x3, local copies, waits for them, and re-layouts: 3.92 us -> 2.14 us
where the time goes in v4:
time: 149 us
  Pallas kernels  145 us (97%)
  local copies, waits for them, and re-layouts  2.14 us (1%)
  between operations  1.93 us (1%)
    pallas_call x1, Pallas kernels, on_device(): pl.pallas_call(kernel, out_shape=(jax.ShapeDtypeStruct((ROWS,), F32), jax...  145 us

profile of v4, /device:TPU:1, one launch (start us, length us, event | category | flops | bytes accessed | tf_op | source)
XLA Modules:
  0.0 149.0 jit_solution(5681581653710915043)
XLA Ops:
  1.9 145.0 %shard_map.67 = (f32[128]{0:T(128)S(1)}, f32[128,1152]{1,0:T(8,128)S(1)}, f32[128,1152]{1,0:T(8,128)S(1)}) custom-call(f32[128,1152]{1,0:T(8,128)} %img_ref.1, f32[128,1152]{1,0:T(8,128)} %txt_ref.1, f32[1]{0:T(128)S(6)} %copy.10.ls_ref, f32[1]{0:T(128)S(6)} %copy.11.bias_ref), custom_call_target="tpu_custom_call" | custom-call | tf_op jit(solution)/shard_map/pallas_call | solution.py:507
  146.9 0.5 copy.12
  147.4 0.8 copy.13
  148.2 0.8 copy.14

commit v5 on v4

--- a/solution.py
+++ b/solution.py
@@ -25,7 +25,7 @@
     emb, early, ring, late_r, late_y, acc, loss_acc, relay, xbuf,
     in_sem, ring_s, ring_r, next_s, next_r, prev_s, prev_r, sib_s, sib_r,
     fy_s, fy_r, rs_s, rs_r, ys_s, ys_r,
-    scat_s, scat_r, wrap_s, wrap_r, own_s, flow_s, flow_r, drop_s, xtra_r,
+    scat_s, scat_r, wrap_s, wrap_r, flow_s, flow_r, drop_s, xtra_r,
 ):
     blk, grp = lax.axis_index("blk"), lax.axis_index("grp")
     zhi, core = grp // 2, grp % 2
@@ -47,10 +47,10 @@
     role = core + zhi - 2 * core * zhi
     inner = ((place + 1) // 256) * (1 - place // 257)
     outer = (511 - place) // 511 + place // 511
-    carrier = (xy % 8) // 4
+    mover = ((xy + 4) // 8) % 2
+    carrier = mover * ((xy % 4) // 2)
     mid = ((z + 1) // 16) * (1 - z // 17)
-    itself = inner * (1 - zhi)
-    dropping = carrier * mid * (1 - itself) == 1
+    dropping = carrier * mid == 1
     gone = (z, NZ - 1 - z)
 
     at_lo, at_hi = xy == 0, xy == 15
@@ -77,29 +77,27 @@
 
     for dev in (up, down, after, before, sibling):
         greet(dev)
-    count = 7 + 14 * (xy // 15) + 14 * ((15 - xy) // 15) + carrier * mid * (1 - itself)
+    count = 5 + 8 * (xy // 15) + 8 * ((15 - xy) // 15) + 2 * mover + carrier * mid
     for k in range(2):
-        is_end = xy == ends[k]
-
-        @pl.when(jnp.logical_not(is_end))
+        @pl.when(mover == 1)
         def _():
             greet(at_place(plane + ends[k]))
 
         @pl.when(xy == ends[1 - k])
         def _():
             def one(c, _):
-                greet(at_place(planes[k] + c + k))
+                greet(at_place((planes[k] + 4 + c) % 512))
                 return _
 
-            lax.fori_loop(0, 15, one, 0)
+            lax.fori_loop(0, 8, one, 0)
 
     @pl.when(inner == 1)
     def _():
         def one(v, _):
-            greet(at_place(plane + (v // 4) * 8 + 4 + v % 4))
+            greet(at_place(plane + (v // 2) * 4 + 6 + v % 2))
             return _
 
-        lax.fori_loop(0, 7 + zhi, one, 0)
+        lax.fori_loop(0, 4, one, 0)
 
     for copy, i, h in loads:
         copy.wait()
@@ -144,10 +142,10 @@
     xtra_to_sib = remote(early.at[XTRA], early.at[EDGE], sib_s.at[1], sib_r.at[1], sibling)
 
     def unit_of(slot, u):
-        return early.at[slot, u // 8, pl.ds(pl.multiple_of((u % 8) * 16, 16), 16)]
+        return early.at[slot, u // 4, pl.ds(pl.multiple_of((u % 4) * 32, 32), 32)]
 
     def scatter(k, c):
-        return remote(unit_of(OWN, c), relay.at[k], scat_s.at[k, c], scat_r.at[k], at_place(plane + c))
+        return remote(unit_of(OWN, c), relay.at[k], scat_s.at[k, c], scat_r.at[k], at_place(plane + 4 + c))
 
     here = (2 + zhi, 3 - zhi)
     there = (2 + ((z + 1) % NZ) // 16, 3 - ((z + NZ - 1) % NZ) // 16)
@@ -155,17 +153,12 @@
     def relayed(k, u, slot):
         return remote(relay.at[k], unit_of(slot, u), wrap_s.at[k], wrap_r.at[k, u], at_place(beyond[k]))
 
-    def straight(k):
-        return remote(
-            unit_of(OWN, ends[k]), unit_of(there[k], ends[k]), own_s.at[k], wrap_r.at[k, ends[k]], at_place(beyond[k])
-        )
-
     def wait_units(k, rows_from):
         def one(v, _):
-            relayed(k, (v // 4) * 8 + rows_from + v % 4, here[k]).wait_recv()
+            relayed(k, (v // 2) * 4 + rows_from + v % 2, here[k]).wait_recv()
             return _
 
-        lax.fori_loop(0, 8, one, 0)
+        lax.fori_loop(0, 4, one, 0)
 
     def on_side(wrapped, fn):
         for k in range(2):
@@ -179,13 +172,11 @@
     for k in range(2):
         @pl.when(xy == ends[k])
         def _():
-            straight(k).start()
-
             def one(c, _):
-                scatter(k, c + k).start()
+                scatter(k, c).start()
                 return _
 
-            lax.fori_loop(0, 15, one, 0)
+            lax.fori_loop(0, 8, one, 0)
 
     @pl.when(jnp.logical_not(wrap_prev))
     def _():
@@ -212,18 +203,14 @@
         )
 
     for k in range(2):
-        @pl.when(xy != ends[k])
-        def _():
-            scatter(k, xy).wait_recv()
-            relayed(k, xy, there[k]).start()
+        @pl.when(mover == 1)
+        def _():
+            scatter(k, xy - 4).wait_recv()
+            relayed(k, xy - 4, there[k]).start()
 
             @pl.when((carrier == 1) & (gone[1 - k] == 0))
             def _():
                 flow(1 - k, relay.at[k]).start()
-
-    @pl.when(place == 511)
-    def _():
-        flow(1, unit_of(OWN, 15)).start()
 
     def forward(h, parts=(0, 2, 1, 3), last=False):
         for j in parts:
@@ -239,14 +226,14 @@
                 flow(d).start()
 
     def xtra_rows(d, v):
-        return pl.ds(pl.multiple_of((d + zhi - 2 * d * zhi) * half + (v % 4) * 16, 16), 16)
+        return pl.ds(pl.multiple_of((d + zhi - 2 * d * zhi) * half + (v % 2) * 32, 32), 32)
 
     def drop(d, v):
         return remote(
-            xbuf.at[d], early.at[XTRA, v // 4, xtra_rows(d, v)], drop_s.at[d], xtra_r.at[d, v], at_place(z + 240)
+            xbuf.at[d], early.at[XTRA, v // 2, xtra_rows(d, v)], drop_s.at[d], xtra_r.at[d, v], at_place(z + 240)
         )
 
-    mine = (xy // 8) * 4 + xy % 4
+    mine = (xy // 4 - 1) * 2 + xy % 2
 
     FRONT, BACK = (0, 1), (2, 3)
     forward(1, FRONT)
@@ -257,7 +244,7 @@
             for d in range(2):
                 to_before(d, j).wait_recv()
 
-    on_side(wrap_next, lambda k: wait_units(k, 4))
+    on_side(wrap_next, lambda k: wait_units(k, 2))
     for j in BACK:
         for d in range(2):
             hop(0, d, j, first=True).start()
@@ -306,7 +293,7 @@
 
     def all_units(k):
         wait_units(k, 0)
-        wait_units(k, 4)
+        wait_units(k, 2)
 
     on_side(wrap_prev, all_units)
 
@@ -394,10 +381,6 @@
         def _():
             drop(d, mine).start()
 
-        @pl.when(itself == 1)
-        def _():
-            early[XTRA, 1, pl.ds(d * half + 48, 16), :] = xbuf[d]
-
     @pl.when(inner == 1)
     def _():
         for d in range(2):
@@ -405,7 +388,7 @@
                 drop(d, v).wait_recv()
                 return _
 
-            lax.fori_loop(0, 7 + zhi, one, 0)
+            lax.fori_loop(0, 4, one, 0)
 
         @pl.when(role == 0)
         def _():
@@ -476,17 +459,15 @@
     for k in range(2):
         @pl.when(xy == ends[k])
         def _():
-            straight(k).wait_send()
-
             def one(c, _):
-                scatter(k, c + k).wait_send()
+                scatter(k, c).wait_send()
                 return _
 
-            lax.fori_loop(0, 15, one, 0)
-
-        @pl.when(xy != ends[k])
-        def _():
-            relayed(k, xy, there[k]).wait_send()
+            lax.fori_loop(0, 8, one, 0)
+
+        @pl.when(mover == 1)
+        def _():
+            relayed(k, xy - 4, there[k]).wait_send()
 
     for d in range(2):
         @pl.when((carrier == 1) & (gone[d] <= 15))
@@ -521,8 +502,8 @@
             pltpu.VMEM((2, 2 * ROWS, WIDTH), BF16),
             pltpu.VMEM((2, ROWS, WIDTH), F32),
             pltpu.VMEM((ROWS, ROWS), F32),
-            pltpu.VMEM((2, 16, WIDTH), BF16),
-            pltpu.VMEM((2, 16, WIDTH), BF16),
+            pltpu.VMEM((2, 32, WIDTH), BF16),
+            pltpu.VMEM((2, 32, WIDTH), BF16),
             dma((2, 2)),
             dma((16, 2, CHUNKS)), dma((16, 2, CHUNKS)),
             dma((2, CHUNKS)), dma((2, CHUNKS)),
@@ -531,8 +512,8 @@
             dma((2, CHUNKS)), dma((2, CHUNKS)),
             dma((2, CHUNKS)), dma((2, CHUNKS)),
             dma((2, CHUNKS)), dma((2, CHUNKS)),
-            dma((2, 16)), dma((2,)), dma((2,)), dma((2, 16)), dma((2,)),
-            dma((2,)), dma((2,)), dma((2,)), dma((2, 8)),
+            dma((2, 8)), dma((2,)), dma((2,)), dma((2, 8)),
+            dma((2,)), dma((2,)), dma((2,)), dma((2, 4)),
         ],
         compiler_params=pltpu.CompilerParams(
             collective_id=0, has_side_effects=True, vmem_limit_bytes=55050240

time: 149 us -> 151 us (1.013)
  no operation moved by 1% of the time
where the time goes in v5:
time: 151 us; the launch traced here: 150 us
  Pallas kernels  146 us (97%)
  local copies, waits for them, and re-layouts  2.14 us (1%)
  between operations  1.93 us (1%)
    pallas_call x1, Pallas kernels, on_device(): pl.pallas_call(kernel, out_shape=(jax.ShapeDtypeStruct((ROWS,), F32), jax...  146 us

profile of v5, /device:TPU:1, one launch (start us, length us, event | category | flops | bytes accessed | tf_op | source)
XLA Modules:
  0.0 149.8 jit_solution(6980115513490554645)
XLA Ops:
  1.9 145.7 %shard_map.67 = (f32[128]{0:T(128)S(1)}, f32[128,1152]{1,0:T(8,128)S(1)}, f32[128,1152]{1,0:T(8,128)S(1)}) custom-call(f32[128,1152]{1,0:T(8,128)} %img_ref.1, f32[128,1152]{1,0:T(8,128)} %txt_ref.1, f32[1]{0:T(128)S(6)} %copy.10.ls_ref, f32[1]{0:T(128)S(6)} %copy.11.bias_ref), custom_call_target="tpu_custom_call" | custom-call | tf_op jit(solution)/shard_map/pallas_call | solution.py:488
  147.6 0.5 copy.12
  148.1 0.8 copy.13
  149.0 0.8 copy.14

commit v6 on v4

--- a/solution.py
+++ b/solution.py
@@ -52,6 +52,7 @@
     itself = inner * (1 - zhi)
     dropping = carrier * mid * (1 - itself) == 1
     gone = (z, NZ - 1 - z)
+    ahead = 1 - (xy % 12 + 11) // 12
 
     at_lo, at_hi = xy == 0, xy == 15
     wrap_next = xy == 15 * (1 - zhi)
@@ -108,8 +109,6 @@
             x = emb[i, r, :]
             inv = lax.rsqrt(jnp.sum(x * x, axis=1, keepdims=True) + 1e-06)
             early[OWN, i, r, :] = (x * inv).astype(BF16)
-    acc[...] = jnp.zeros_like(acc)
-    loss_acc[...] = jnp.zeros_like(loss_acc)
     scale = jnp.exp(jnp.full((1, 128), ls_ref[0], F32))
     offset = bias_ref[0]
 
@@ -250,6 +249,10 @@
 
     FRONT, BACK = (0, 1), (2, 3)
     forward(1, FRONT)
+
+    @pl.when(ahead == 1)
+    def _():
+        forward(2, FRONT)
 
     @pl.when(jnp.logical_not(wrap_next))
     def _():
@@ -280,11 +283,13 @@
             loss_acc[...] += jnp.maximum(u, 0.0) + jnp.log1p(e)
 
     def skewed(h, _):
-        forward(h, FRONT)
+        forward(h + ahead, FRONT)
         forward(h - 1, BACK)
         forward_xtra(h - 1)
         return _
 
+    acc[...] = jnp.zeros_like(acc)
+    loss_acc[...] = jnp.zeros_like(loss_acc)
     lax.fori_loop(2, 6, skewed, 0)
     forward(5, BACK)
     forward_xtra(5)
@@ -318,7 +323,16 @@
         diagonal = jnp.where(p == 0, 1.0, 0.0).astype(F32)
         used = inner * (p // 3) == 0
         for i in range(2):
-            forward(6 + 2 * p + i)
+            if i == 0:
+                @pl.when((p == 0) & (ahead == 1))
+                def _():
+                    forward(6, BACK)
+
+                @pl.when((p > 0) | (ahead == 0))
+                def _():
+                    forward(6 + 2 * p)
+            else:
+                forward(7 + 2 * p)
             forward_xtra(6 + 2 * p + i)
 
             @pl.when(used)

time: 149 us -> 150 us (level)
  no operation moved by 1% of the time
where the time goes in v6:
time: 150 us; the launch traced here: 149 us
  Pallas kernels  145 us (97%)
  local copies, waits for them, and re-layouts  2.14 us (1%)
  between operations  1.93 us (1%)
    pallas_call x1, Pallas kernels, on_device(): pl.pallas_call(kernel, out_shape=(jax.ShapeDtypeStruct((ROWS,), F32), jax...  145 us

profile of v6, /device:TPU:1, one launch (start us, length us, event | category | flops | bytes accessed | tf_op | source)
XLA Modules:
  0.0 149.0 jit_solution(14222964891824734383)
XLA Ops:
  1.9 145.0 %shard_map.67 = (f32[128]{0:T(128)S(1)}, f32[128,1152]{1,0:T(8,128)S(1)}, f32[128,1152]{1,0:T(8,128)S(1)}) custom-call(f32[128,1152]{1,0:T(8,128)} %img_ref.1, f32[128,1152]{1,0:T(8,128)} %txt_ref.1, f32[1]{0:T(128)S(6)} %copy.10.ls_ref, f32[1]{0:T(128)S(6)} %copy.11.bias_ref), custom_call_target="tpu_custom_call" | custom-call | tf_op jit(solution)/shard_map/pallas_call | solution.py:521
  146.9 0.5 copy.12
  147.4 0.8 copy.13
  148.2 0.8 copy.14
